TPU v7x, 32 devices: a whole 2x2x4 slice. The times are simulated.
32 devices in a mesh: seq: 8 (over z, x), head: 4 (over y, core).
Axes of the slice: x: 2, y: 2, z: 4, core: 2. Of those that a mesh axis runs over, the one named last changes fastest.
Arguments:
- block_input: float32 [8, 4096, 768], P('head', 'seq'), may hold values from -6 to 6
- cotangent: float32 [8, 4096, 768], P('head', 'seq'), may hold values from -6 to 6
- w_z: float32 [768, 1536], P(('seq', 'head')), may hold values from -0.21875 to 0.21875
- w_x: float32 [768, 1536], P(('seq', 'head')), may hold values from -1 to 1
- w_bc: float32 [768, 256], P(('seq', 'head')), may hold values from -0.21875 to 0.21875
- w_dt: float32 [768, 24], P(('seq', 'head')), may hold values from -0.21875 to 0.21875
- w_out: float32 [1536, 768], P(('seq', 'head')), may hold values from -0.15625 to 0.15625
- mom_z: float32 [768, 1536], P(('seq', 'head')), may hold values from -320 to 320
- mom_x: float32 [768, 1536], P(('seq', 'head')), may hold values from -320 to 320
- mom_bc: float32 [768, 256], P(('seq', 'head')), may hold values from -320 to 320
- mom_dt: float32 [768, 24], P(('seq', 'head')), may hold values from -320 to 320
- mom_out: float32 [1536, 768], P(('seq', 'head')), may hold values from -1024 to 1024
- small_params: float32 [11336], replicated, may hold values from -7 to 3, as said below
- small_moment: float32 [11336], replicated, may hold values from -320 to 320
Outputs:
- block_output: float32 [8, 4096, 768], P('head', 'seq')
- input_grad: float32 [8, 4096, 768], P('head', 'seq')
- new_w_z: float32 [768, 1536], P(('seq', 'head'))
- new_w_x: float32 [768, 1536], P(('seq', 'head'))
- new_w_bc: float32 [768, 256], P(('seq', 'head'))
- new_w_dt: float32 [768, 24], P(('seq', 'head'))
- new_w_out: float32 [1536, 768], P(('seq', 'head'))
- new_mom_z: float32 [768, 1536], P(('seq', 'head'))
- new_mom_x: float32 [768, 1536], P(('seq', 'head'))
- new_mom_bc: float32 [768, 256], P(('seq', 'head'))
- new_mom_dt: float32 [768, 24], P(('seq', 'head'))
- new_mom_out: float32 [1536, 768], P(('seq', 'head'))
- new_small_moment: float32 [11336], replicated
- new_small_params: float32 [11336], replicated
Inputs may be any that keep to these rules, and one draw needn't show every extreme that they name: `small_params`: log_rates in [0, 2.77], step_bias in [-6.9, -2.3], skip in [0.5, 1.5].
All inputs are finite; a program needn't handle non-finite values.
Results may differ from a plain program's by a relative error of at most 0.012.
The roundings to bfloat16 on the way count: a program that leaves them out, or rounds other values in their place, can miss the bound.
Values may be sent and summed in bfloat16 or wider, within the bound.
A program may use at most 256 MiB of HBM per device.

v0:
```python
from functools import partial
import math

import jax
import jax.numpy as jnp
from jax import lax
from jax.sharding import PartitionSpec as P

D = 768
H = 24
HP = 64
NS = 128
CONV = 4
SPAN = 256
DI = 1536
XC = 1792


EPS = 1e-05
HIGH = lax.Precision.HIGHEST
MOMENTUM = 0.95
RATE = 0.2
DECAY = 0.1
SMALL_MOMENTUM = 0.9
SMALL_RATE = 0.1
COEF_A = 3.4445
COEF_B = -4.775
COEF_C = 2.0315


def kind_lengths():
    return (D, CONV * XC, XC, H, H, H, DI)


def unpack(smalls):
    pieces = []
    offset = 0
    for length in kind_lengths():
        pieces.append(smalls[offset : offset + length])
        offset = offset + length
    norm_gain, conv_flat, conv_bias, log_rates, skip_factor, step_bias, gate_gain = pieces
    return (
        norm_gain,
        conv_flat.reshape(CONV, XC),
        conv_bias,
        log_rates,
        skip_factor,
        step_bias,
        gate_gain,
    )


def causal_conv(values, weight, bias_vec):
    length = values.shape[0]
    taps = weight.shape[0]
    padded = jnp.pad(values, ((taps - 1, 0), (0, 0)))
    running = bias_vec[None, :] + weight[0][None, :] * padded[0:length]
    for offset in range(1, taps):
        running = running + weight[offset][None, :] * padded[offset : offset + length]
    return running


def span_step(carry_state, input_values, rates):
    x_block, dt_block, b_block, c_block = input_values
    cumul = jnp.cumsum(dt_block * rates[None, :], axis=0).T
    scores = jnp.dot(c_block, b_block.T, precision=HIGH)
    size = cumul.shape[1]
    causal = jnp.arange(size)[:, None] >= jnp.arange(size)[None, :]
    differ = cumul[:, :, None] - cumul[:, None, :]
    decays = jnp.exp(jnp.where(causal[None], differ, -jnp.inf)) * scores[None]
    inner = jnp.einsum("hij,jh,jhp->ihp", decays, dt_block, x_block, precision=HIGH)
    carried = (
        jnp.einsum("in,hpn->ihp", c_block, carry_state, precision=HIGH)
        * jnp.exp(cumul.T)[:, :, None]
    )
    weights_tail = jnp.exp(cumul[:, -1][None, :] - cumul.T) * dt_block
    fresh = jnp.einsum("jh,jn,jhp->hpn", weights_tail, b_block, x_block, precision=HIGH)
    new_state = jnp.exp(cumul[:, -1])[:, None, None] * carry_state + fresh
    return (new_state, inner + carried)


def scan_ssd(heads_x, steps_dt, b_mat, c_mat, rates):
    length, head_count, width = heads_x.shape
    blocks = length // SPAN
    input_values = (
        heads_x.reshape(blocks, SPAN, head_count, width),
        steps_dt.reshape(blocks, SPAN, head_count),
        b_mat.reshape(blocks, SPAN, -1),
        c_mat.reshape(blocks, SPAN, -1),
    )
    initial_state = jnp.zeros((head_count, width, b_mat.shape[1]), jnp.float32)
    stepper = jax.checkpoint(partial(span_step, rates=rates))
    final_state, outputs = lax.scan(stepper, initial_state, input_values)
    return outputs.reshape(length, head_count, width)


def mixer_local(
    z_part,
    x_part,
    timestep_portion,
    bc_full,
    conv_weight,
    conv_bias,
    log_rates,
    skip_factor,
    step_bias,
):
    length = x_part.shape[0]
    head_count = log_rates.shape[0]
    x_conv = jax.nn.silu(causal_conv(x_part, conv_weight, conv_bias))
    heads_x = x_conv.reshape(length, head_count, -1)
    steps_dt = jax.nn.softplus(timestep_portion + step_bias[None, :])
    half = bc_full.shape[1] // 2
    ssd_out = scan_ssd(heads_x, steps_dt, bc_full[:, :half], bc_full[:, half:], -jnp.exp(log_rates))
    mixed = (ssd_out + skip_factor[None, :, None] * heads_x).reshape(length, -1)
    return mixed * jax.nn.silu(z_part)


def bc_local(bc_part, conv_weight, conv_bias):
    return jax.nn.silu(causal_conv(bc_part, conv_weight, conv_bias))


def newton_schulz(batch):
    norms = jnp.sqrt(jnp.sum(batch * batch, axis=(1, 2), keepdims=True))
    matrix = batch / (norms + 1e-07)
    for sweep_index in range(5):
        gram = jnp.einsum("bik,bjk->bij", matrix, matrix, precision=HIGH)
        poly = COEF_B * gram + COEF_C * jnp.einsum("bij,bjk->bik", gram, gram, precision=HIGH)
        matrix = COEF_A * matrix + jnp.einsum("bij,bjk->bik", poly, matrix, precision=HIGH)
    return matrix


def small_step(params, moment):
    pieces = []
    offset = 0
    for length in kind_lengths():
        segment = moment[offset : offset + length]
        pieces.append(segment * lax.rsqrt(jnp.mean(segment * segment) + 1e-06))
        offset = offset + length
    return params - SMALL_RATE * jnp.concatenate(pieces)


def place_in(shape, piece, corner):
    return lax.dynamic_update_slice(jnp.zeros(shape, jnp.float32), piece, corner)


def body(
    block_input,
    cotangent,
    w_z,
    w_x,
    w_bc,
    w_dt,
    w_out,
    mom_z,
    mom_x,
    mom_bc,
    mom_dt,
    mom_out,
    small_params,
    small_moment,
):
    n_head = lax.axis_size("head")
    head_position = lax.axis_index("head")
    flat_idx = lax.axis_index(("seq", "head"))
    heads_here = H // n_head
    chans = DI // n_head
    bc_here = 2 * NS // n_head
    ch_start = head_position * chans
    bc_start = head_position * bc_here
    hd_start = head_position * heads_here
    zero_idx = jnp.int32(0)
    norm_gain, conv_taps, conv_bias, log_rates, skip_factor, step_bias, gate_gain = unpack(
        small_params
    )
    full_z, full_x, full_bc, full_dt, full_out = (
        lax.all_gather(w_z.astype(jnp.bfloat16), ("seq", "head"), axis=0, tiled=True),
        lax.all_gather(w_x.astype(jnp.bfloat16), ("seq", "head"), axis=0, tiled=True),
        lax.all_gather(w_bc.astype(jnp.bfloat16), ("seq", "head"), axis=0, tiled=True),
        lax.all_gather(w_dt.astype(jnp.bfloat16), ("seq", "head"), axis=0, tiled=True),
        lax.all_gather(w_out.astype(jnp.bfloat16), ("seq", "head"), axis=0, tiled=True),
    )
    w_in_here = jnp.concatenate(
        [
            lax.dynamic_slice_in_dim(full_z, ch_start, chans, 1),
            lax.dynamic_slice_in_dim(full_x, ch_start, chans, 1),
            lax.dynamic_slice_in_dim(full_bc, bc_start, bc_here, 1),
            lax.dynamic_slice_in_dim(full_dt, hd_start, heads_here, 1),
        ],
        axis=1,
    )
    local_output_weight = lax.dynamic_slice_in_dim(full_out, ch_start, chans, 0)
    inv_rms = lax.rsqrt(jnp.mean(block_input * block_input, axis=-1, keepdims=True) + EPS)
    unit = block_input * inv_rms
    normed = (unit * norm_gain).astype(jnp.bfloat16)
    cot_local = cotangent.astype(jnp.bfloat16)
    gathered, cotangent_row_slice = (
        lax.all_gather(normed, "head", axis=0, tiled=True),
        lax.all_gather(cot_local, "head", axis=0, tiled=True),
    )
    proj_rows = jnp.einsum(
        "slk,kc->slc", gathered, w_in_here, preferred_element_type=jnp.float32
    ).astype(jnp.bfloat16)
    whole = lax.all_to_all(proj_rows, "seq", split_axis=0, concat_axis=1, tiled=True)[0]
    z_part = whole[:, :chans].astype(jnp.float32)
    x_part = whole[:, chans : 2 * chans].astype(jnp.float32)
    bc_part = whole[:, 2 * chans : 2 * chans + bc_here].astype(jnp.float32)
    timestep_portion = whole[:, 2 * chans + bc_here :].astype(jnp.float32)
    conv_w_x = lax.dynamic_slice_in_dim(conv_taps, ch_start, chans, 1)
    conv_b_x = lax.dynamic_slice_in_dim(conv_bias, ch_start, chans, 0)
    conv_w_bc = lax.dynamic_slice_in_dim(conv_taps, DI + bc_start, bc_here, 1)
    conv_b_bc = lax.dynamic_slice_in_dim(conv_bias, DI + bc_start, bc_here, 0)
    rates_here = lax.dynamic_slice_in_dim(log_rates, hd_start, heads_here, 0)
    skip_here = lax.dynamic_slice_in_dim(skip_factor, hd_start, heads_here, 0)
    stepb_here = lax.dynamic_slice_in_dim(step_bias, hd_start, heads_here, 0)
    gate_here = lax.dynamic_slice_in_dim(gate_gain, ch_start, chans, 0)
    bc_act, bc_pull = jax.vjp(bc_local, bc_part, conv_w_bc, conv_b_bc)
    bc_full = lax.all_gather(bc_act.astype(jnp.bfloat16), "head", axis=1, tiled=True).astype(
        jnp.float32
    )
    gated, gated_pull = jax.vjp(
        mixer_local,
        z_part,
        x_part,
        timestep_portion,
        bc_full,
        conv_w_x,
        conv_b_x,
        rates_here,
        skip_here,
        stepb_here,
    )
    total_sq = lax.psum(jnp.sum(gated * gated, axis=-1), "head")
    inv_gate = lax.rsqrt(total_sq / DI + EPS)[:, None]
    outgate = (gated * inv_gate * gate_here).astype(jnp.bfloat16)
    token_gate = lax.all_to_all(outgate[None], "seq", split_axis=1, concat_axis=0, tiled=True)
    current_rows = token_gate
    branch = lax.psum_scatter(
        jnp.einsum(
            "amt,tp->amp", current_rows, local_output_weight, preferred_element_type=jnp.float32
        ).astype(jnp.bfloat16),
        "head",
        scatter_dimension=0,
        tiled=True,
    ).astype(jnp.float32)
    grad_out_term = place_in(
        (DI, D),
        jnp.einsum(
            "gry,grp->yp", token_gate, cotangent_row_slice, preferred_element_type=jnp.float32
        ),
        (ch_start, zero_idx),
    )
    d_tok = jnp.einsum(
        "omk,ek->ome", cotangent_row_slice, local_output_weight, preferred_element_type=jnp.float32
    ).astype(jnp.bfloat16)
    block_output = block_input + branch
    d_gate = lax.all_to_all(d_tok, "seq", split_axis=0, concat_axis=1, tiled=True)[0].astype(
        jnp.float32
    )
    d_gate_gain = jnp.sum(d_gate * gated * inv_gate, axis=0)
    d_scaled = d_gate * gate_here
    inner = lax.psum(jnp.sum(d_scaled * gated, axis=-1), "head")
    d_gated = inv_gate * d_scaled - gated * inv_gate**3 * (inner / DI)[:, None]
    d_z, d_x, d_dt, d_bc_full, d_cw_x, d_cb_x, d_rates, d_skip, d_stepb = gated_pull(d_gated)
    d_bc_own = lax.psum_scatter(d_bc_full, "head", scatter_dimension=1, tiled=True)
    d_bc_part, d_cw_bc, d_cb_bc = bc_pull(d_bc_own)
    d_whole = jnp.concatenate([d_z, d_x, d_bc_part, d_dt], axis=-1).astype(jnp.bfloat16)
    d_rows = lax.all_to_all(d_whole[None], "seq", split_axis=1, concat_axis=0, tiled=True)
    grad_in_here = jnp.einsum("slk,slc->kc", gathered, d_rows, preferred_element_type=jnp.float32)
    current_rows = d_rows
    d_normed = lax.psum_scatter(
        jnp.einsum("slc,kc->slk", current_rows, w_in_here, preferred_element_type=jnp.float32),
        "head",
        scatter_dimension=0,
        tiled=True,
    )
    g_z = place_in((D, DI), grad_in_here[:, :chans], (zero_idx, ch_start))
    g_x = place_in((D, DI), grad_in_here[:, chans : 2 * chans], (zero_idx, ch_start))
    g_bc = place_in(
        (D, 2 * NS), grad_in_here[:, 2 * chans : 2 * chans + bc_here], (zero_idx, bc_start)
    )
    g_dt = place_in((D, H), grad_in_here[:, 2 * chans + bc_here :], (zero_idx, hd_start))
    d_norm_gain = jnp.sum(d_normed * unit, axis=(0, 1))
    d_unit = d_normed * norm_gain
    input_grad = cotangent + inv_rms * (
        d_unit - unit * jnp.mean(d_unit * unit, axis=-1, keepdims=True)
    )
    rows_in = mom_z.shape[0]
    rows_out = mom_out.shape[0]
    in_at = flat_idx * rows_in
    out_at = flat_idx * rows_out
    term_z = g_z + place_in((D, DI), MOMENTUM * mom_z, (in_at, zero_idx))
    term_x = g_x + place_in((D, DI), MOMENTUM * mom_x, (in_at, zero_idx))
    term_bc = g_bc + place_in((D, 2 * NS), MOMENTUM * mom_bc, (in_at, zero_idx))
    term_dt = g_dt + place_in((D, H), MOMENTUM * mom_dt, (in_at, zero_idx))
    conv_grad = place_in((CONV, XC), d_cw_x, (zero_idx, ch_start)) + place_in(
        (CONV, XC), d_cw_bc, (zero_idx, DI + bc_start)
    )
    convb_grad = place_in((XC,), d_cb_x, (ch_start,)) + place_in((XC,), d_cb_bc, (DI + bc_start,))
    small_term = jnp.concatenate(
        [
            d_norm_gain,
            conv_grad.reshape(-1),
            convb_grad,
            place_in((H,), d_rates, (hd_start,)),
            place_in((H,), d_skip, (hd_start,)),
            place_in((H,), d_stepb, (hd_start,)),
            place_in((DI,), d_gate_gain, (ch_start,)),
        ]
    )
    factor = 0.2 * math.sqrt(D)
    keep = 1.0 - RATE * DECAY

    def own_rows(matrix, at, count):
        return lax.dynamic_slice_in_dim(matrix, at, count, 0)

    term_out = grad_out_term + place_in((DI, D), MOMENTUM * mom_out, (out_at, zero_idx))
    sum_z, sum_x, sum_bc, sum_dt, sum_out, sum_small = lax.psum(
        (term_z, term_x, term_bc, term_dt, term_out, small_term), ("seq", "head")
    )
    z_blocks = sum_z.reshape(D, H, HP).transpose(1, 2, 0)
    x_blocks = sum_x.reshape(D, H, HP).transpose(1, 2, 0)
    out_blocks = sum_out.reshape(H, HP, D)
    ortho = newton_schulz(jnp.concatenate([z_blocks, x_blocks, out_blocks], axis=0))
    ortho_z = ortho[:H].transpose(2, 0, 1).reshape(D, DI)
    ortho_x = ortho[H : 2 * H].transpose(2, 0, 1).reshape(D, DI)
    ortho_out = ortho[2 * H :].reshape(DI, D)
    ortho_bc = newton_schulz(sum_bc.T[None])[0].T
    ortho_dt = newton_schulz(sum_dt.T[None])[0].T
    new_w_z = w_z * keep - RATE * factor * own_rows(ortho_z, in_at, rows_in)
    new_w_x = w_x * keep - RATE * factor * own_rows(ortho_x, in_at, rows_in)
    new_w_bc = w_bc * keep - RATE * factor * own_rows(ortho_bc, in_at, rows_in)
    new_w_dt = w_dt * keep - RATE * factor * own_rows(ortho_dt, in_at, rows_in)
    new_w_out = w_out * keep - RATE * factor * own_rows(ortho_out, out_at, rows_out)
    mom_z_new = own_rows(sum_z, in_at, rows_in)
    mom_x_new = own_rows(sum_x, in_at, rows_in)
    mom_bc_new = own_rows(sum_bc, in_at, rows_in)
    mom_dt_new = own_rows(sum_dt, in_at, rows_in)
    mom_out_new = own_rows(sum_out, out_at, rows_out)
    new_small_moment = SMALL_MOMENTUM * small_moment + sum_small
    new_small_params = small_step(small_params, new_small_moment)
    return (
        block_output,
        input_grad,
        new_w_z,
        new_w_x,
        new_w_bc,
        new_w_dt,
        new_w_out,
        mom_z_new,
        mom_x_new,
        mom_bc_new,
        mom_dt_new,
        mom_out_new,
        new_small_moment,
        new_small_params,
    )


def solution(mesh):
    return jax.shard_map(
        body,
        mesh=mesh,
        in_specs=(
            P("head", "seq", None),
            P("head", "seq", None),
            P(("seq", "head"), None),
            P(("seq", "head"), None),
            P(("seq", "head"), None),
            P(("seq", "head"), None),
            P(("seq", "head"), None),
            P(("seq", "head"), None),
            P(("seq", "head"), None),
            P(("seq", "head"), None),
            P(("seq", "head"), None),
            P(("seq", "head"), None),
            P(),
            P(),
        ),
        out_specs=(
            P("head", "seq", None),
            P("head", "seq", None),
            P(("seq", "head"), None),
            P(("seq", "head"), None),
            P(("seq", "head"), None),
            P(("seq", "head"), None),
            P(("seq", "head"), None),
            P(("seq", "head"), None),
            P(("seq", "head"), None),
            P(("seq", "head"), None),
            P(("seq", "head"), None),
            P(("seq", "head"), None),
            P(),
            P(),
        ),
        check_vma=False,
    )
```

profile of v0, /device:TPU:0, one launch (start us, length us, event | category | flops | bytes accessed | tf_op | source)
XLA Modules:
  0.0 3017.6 jit_solution(5107844922361011021)
XLA Ops:
  15.6 55.9 %all-gather.15.cloned.1.call-done = bf16[1536,768]{1,0:T(8,128)(2,1)} async-done(((bf16[48,768]{1,0:T(8,128)(2,1)}), bf16[1536,768]{1,0:T(8,128)(2,1)}) %all-gather.15.cloned.1.call-update) | async-done | bytes 2359312 | tf_op jit(solution)/shard_map/all_gather | solution.py:181
  71.6 47.4 %all-gather.17.cloned.1.call-done = bf16[8,512,768]{2,1,0:T(8,128)(2,1)} async-done(((bf16[2,512,768]{2,1,0:T(8,128)(2,1)}), bf16[8,512,768]{2,1,0:T(8,128)(2,1)}) %all-gather.17.cloned.1.call-update) | async-done | bytes 6291472 | tf_op jit(solution)/shard_map/all_gather | solution.py:199
  132.0 90.6 %all_gather.28 = bf16[768,24]{1,0:T(8,128)(2,1)S(1)} all-gather(bf16[24,24]{1,0:T(8,128)(2,1)S(1)} %convert_element_type.79), channel_id=1, replica_groups=mesh['seq'=8,'head'=4] {'seq','head'}, dimensions={0}, use_global_device_ids=true | all-gather | bytes 38016 | tf_op jit(solution)/shard_map/all_gather | solution.py:180
  222.9 46.9 %all_gather.27 = bf16[768,256]{1,0:T(8,128)(2,1)S(1)} all-gather(bf16[24,256]{1,0:T(8,128)(2,1)S(1)} %convert_element_type.78), channel_id=1, replica_groups=mesh['seq'=8,'head'=4] {'seq','head'}, dimensions={0}, use_global_device_ids=true | all-gather | bytes 405504 | tf_op jit(solution)/shard_map/all_gather | solution.py:179
  291.2 43.2 %all-gather.7.cloned.1.call-done = bf16[8,512,768]{2,1,0:T(8,128)(2,1)} async-done(((bf16[2,512,768]{2,1,0:T(8,128)(2,1)}), bf16[8,512,768]{2,1,0:T(8,128)(2,1)}) %all-gather.7.cloned.1.call-update) | async-done | bytes 6291472 | tf_op jit(solution)/shard_map/all_gather | solution.py:198
  372.6 128.4 %all-to-all-done = bf16[8,512,838]{1,2,0:T(8,128)(2,1)} async-done(((bf16[8,512,838]{1,2,0:T(8,128)(2,1)}), bf16[8,512,838]{1,2,0:T(8,128)(2,1)}, u32[]{:S(2)}, u32[]{:S(2)}) %all-to-all-start) | async-done | bytes 6864928 | tf_op jit(solution)/shard_map/all_to_all | solution.py:204
  555.4 332.7 %while.41 = (s32[]{:T(128)}, f32[6,64,128]{2,1,0:T(8,128)S(1)}, f32[16,256,6,64]{1,0,3,2:T(8,128)}, f32[16,6,64,128]{3,2,1,0:T(8,128)}, f32[16,256,6]{1,2,0:T(8,...) while((s32[]{:T(128)}, f32[6,64,128]{2,1,0:T(8,128)S(1)}, ...), condition=%wide.region_4.5_spmd.clone, body=%wide.region_1.4_spmd.clone.sunk | while | flops 706662912 | bytes 5775769 | solution.py:93
  962.8 582.5 %while.42 = (s32[]{:T(128)}, f32[6]{0:T(128)S(1)}, f32[6,64,128]{2,1,0:T(8,128)S(1)}, f32[16,256,6,64]{1,0,3,2:T(8,128)}, f32[16,256,6]{1,2,0:T(8,128)S(1)}, /*i...) while((s32[]{:T(128)}, f32[6]{0:T(128)S(1)}, ...), condition=%wide.region_22.23_spmd.clone, body=%wide.region_10.22_spmd.clone.sunk | while | flops 1667676160 | bytes 14942984 | solution.py:93
  1578.5 66.9 %reduce.23 = bf16[4096,384]{1,0:T(8,128)(2,1)S(1)} reduce(bf16[4096,1,384]{2,1,0:T(2,128)(2,1)} %bitcast.535, bf16[]{:T(256)} %broadcast.437), dimensions={1}, to_apply=%bitcast.276.reduce_sub_computation | reduce | bytes 6291458
  1655.0 17.5 multiply_reduce_fusion.9
  1698.0 32.1 %copy.305 = bf16[1,4096,838]{2,0,1:T(2,128)(2,1)} copy(bf16[1,4096,838]{1,2,0:T(8,128)(2,1)} %pad_maximum_fusion.1) | data formatting | bytes 13729792 | tf_op jit(solution)/shard_map/concatenate | solution.py:267
  1730.1 157.8 %reduce.22 = bf16[4096,838]{1,0:T(8,128)(2,1)} reduce(bf16[4096,1,838]{2,1,0:T(2,128)(2,1)} %bitcast.525, bf16[]{:T(256)} %broadcast.437), dimensions={1}, to_apply=%bitcast.278.reduce_sub_computation | reduce | bytes 13729794
  1930.8 127.8 %all-to-all-done.3 = bf16[8,2,214528]{2,1,0:T(2,128)(2,1)} async-done(((bf16[8,2,214528]{2,1,0:T(2,128)(2,1)}), bf16[8,2,214528]{2,1,0:T(2,128)(2,1)}, u32[]{:S(2)}, u32[]{:S(2)}) %all-to-all-start.3) | async-done | bytes 6864928 | tf_op jit(solution)/shard_map/all_to_all | solution.py:268
  2146.5 514.4 %all-reduce.25.cloned.1.call-done = (f32[1536,768]{1,0:T(8,128)}, f32[768,1536]{1,0:T(8,128)}, f32[768,1536]{1,0:T(8,128)}, f32[768,256]{1,0:T(8,128)}, f32[768,24]{0,1:T(8,128)}) async-done(((f32[1536,768]{1,0:T(8,128)}, f32[768,1536]{1,0:T(8,128)}, f32[768,1536]{1,0:T(8,128)}, f32[768,256]{1,0:T(8,128)}, f32[768,24]{0,1:T(8,128)}), (f32[1536,768]{1,0:T(8,128)}, f32[768,1536]{1,0:T(8,128)}, ...) | async-done | bytes 15015952 | tf_op jit(solution)/shard_map/psum | solution.py:318
  2684.5 20.0 fusion.178
  2711.0 22.2 multiply_add_fusion.4
  2750.9 22.2 multiply_add_fusion.3
  2773.1 20.0 fusion.197
  2795.7 23.2 multiply_add_fusion.2
  2819.0 19.9 fusion.199
  2841.6 23.1 multiply_add_fusion.1
  2871.9 19.7 fusion.201
  2894.3 23.2 multiply_add_fusion
  2954.4 41.0 %psum.63 = f32[11336]{0:T(1024)S(1)} all-reduce(f32[11336]{0:T(1024)S(1)} %concatenate.38), channel_id=1, replica_groups=mesh['seq'=8,'head'=4] {'seq','head'}, use_global_device_ids=true, to_apply=%region_49.50 | all-reduce | flops 11336 | bytes 90688 | tf_op jit(solution)/shard_map/psum | solution.py:318
  (1522 shorter events, 1428.2 us)
Async XLA Ops:
  7.2 64.3 %all-gather.15.cloned.1.call-start = ((), (), s32[]{:S(2)}) async-start(), calls=%async_computation.11 | async-start | bytes 2433024 | tf_op jit(solution)/shard_map/all_gather | solution.py:181
  9.0 110.0 %all-gather.17.cloned.1.call-start = ((), (), s32[]{:S(2)}) async-start(), calls=%async_computation.13 | async-start | bytes 7864320 | tf_op jit(solution)/shard_map/all_gather | solution.py:199
  12.3 257.8 %all-gather.9.cloned.1.call-start = ((), (), s32[]{:S(2)}) async-start(), calls=%async_computation.8 | async-start | bytes 2433024 | tf_op jit(solution)/shard_map/all_gather | solution.py:177
  13.0 274.1 %all-gather.11.cloned.1.call-start = ((), (), s32[]{:S(2)}) async-start(), calls=%async_computation.9 | async-start | bytes 2433024 | tf_op jit(solution)/shard_map/all_gather | solution.py:178
  13.7 320.7 %all-gather.7.cloned.1.call-start = ((), (), s32[]{:S(2)}) async-start(), calls=%async_computation.7 | async-start | bytes 7864320 | tf_op jit(solution)/shard_map/all_gather | solution.py:198
  14.1 112.2 %copy-start.37 = (f32[2,512]{1,0:T(2,128)}, f32[2,512]{1,0:T(2,128)S(1)}, u32[]{:S(2)}) copy-start(f32[2,512]{1,0:T(2,128)S(1)} %add_rsqrt_fusion.1) | copy-start | bytes 12292
  126.3 96.5 %copy-start.31 = (f32[24,256]{1,0:T(8,128)S(1)}, f32[24,256]{1,0:T(8,128)}, u32[]{:S(2)}) copy-start(f32[24,256]{1,0:T(8,128)} %param.22) | copy-start | bytes 73732
  126.3 217.9 %all-to-all-start.2 = ((bf16[8,512,384]{1,2,0:T(8,128)(2,1)}), bf16[8,512,384]{1,2,0:T(8,128)(2,1)S(1)}, u32[]{:S(2)}, u32[]{:S(2)}) async-start(bf16[8,512,384]{1,2,0:T(8,128)(2,1)} %convert_bitcast_fusion), calls=%async_computation.3 | async-start | bytes 6291456 | tf_op jit(solution)/shard_map/all_to_all | solution.py:257
  222.8 121.3 %copy-start.54 = (bf16[768,6]{0,1:T(8,128)(2,1)}, bf16[768,6]{0,1:T(8,128)(2,1)S(1)}, u32[]{:S(2)}) copy-start(bf16[768,6]{0,1:T(8,128)(2,1)S(1)} %copy.357) | copy-start | bytes 27652
  270.0 74.2 %copy-start.33 = (bf16[768,64]{0,1:T(8,128)(2,1)}, bf16[768,64]{0,1:T(8,128)(2,1)S(1)}, u32[]{:S(2)}) copy-start(bf16[768,64]{0,1:T(8,128)(2,1)S(1)} %copy.356) | copy-start | bytes 294916
  344.2 156.8 %all-to-all-start = ((bf16[8,512,838]{1,2,0:T(8,128)(2,1)}), bf16[8,512,838]{1,2,0:T(8,128)(2,1)}, u32[]{:S(2)}, u32[]{:S(2)}) async-start(bf16[8,512,838]{1,2,0:T(8,128)(2,1)} %convolution_convert_fusion), calls=%async_computation | async-start | bytes 13762560 | tf_op jit(solution)/shard_map/all_to_all | solution.py:204
  349.7 194.3 %all-gather.13.cloned.1.call-start = ((), (), s32[]{:S(2)}) async-start(), calls=%async_computation.10 | async-start | bytes 2621440 | tf_op jit(solution)/shard_map/all_gather | solution.py:218
  523.2 1165.1 %reduce-scatter.6.cloned.1.call-start = ((), (), s32[]{:S(2)}) async-start(), calls=%async_computation.14 | async-start | bytes 5242880 | tf_op jit(solution)/shard_map/reduce_scatter | solution.py:265
  1649.0 253.6 %all-to-all-start.1 = ((bf16[8,2,98304]{2,1,0:T(2,128)(2,1)}), bf16[8,2,98304]{2,1,0:T(2,128)(2,1)}, u32[]{:S(2)}, u32[]{:S(2)}) async-start(bf16[8,2,98304]{2,1,0:T(2,128)(2,1)} %reshape.755), calls=%async_computation.1 | async-start | bytes 6291456 | tf_op jit(solution)/shard_map/all_to_all | solution.py:236
  1654.9 19.3 copy-start.45
  1655.0 19.3 copy-start.47
  1902.7 155.9 %all-to-all-start.3 = ((bf16[8,2,214528]{2,1,0:T(2,128)(2,1)}), bf16[8,2,214528]{2,1,0:T(2,128)(2,1)}, u32[]{:S(2)}, u32[]{:S(2)}) async-start(bf16[8,2,214528]{2,1,0:T(2,128)(2,1)} %reshape.757), calls=%async_computation.5 | async-start | bytes 13729792 | tf_op jit(solution)/shard_map/all_to_all | solution.py:268
  1908.8 752.1 %all-reduce.25.cloned.1.call-start = ((), (), s32[]{:S(2)}) async-start(), calls=%async_computation.16 | async-start | bytes 30031872 | tf_op jit(solution)/shard_map/psum | solution.py:318
  2121.0 829.9 %reduce-scatter.8.cloned.1.call-start = ((), (), s32[]{:S(2)}) async-start(), calls=%async_computation.15 | async-start | bytes 15728640 | tf_op jit(solution)/shard_map/reduce_scatter | solution.py:271
  2134.0 871.2 %reduce-scatter.4.cloned.1.call-start = ((), (), s32[]{:S(2)}) async-start(), calls=%async_computation.12 | async-start | bytes 7864320 | tf_op jit(solution)/shard_map/reduce_scatter | solution.py:238
  2146.5 520.9 %copy-start.42 = (f32[1792]{0:T(1024)}, f32[1792]{0:T(1024)S(1)}, u32[]{:S(2)}) copy-start(f32[1792]{0:T(1024)S(1)} %add_dynamic-update-slice_fusion.4) | copy-start | bytes 21508
  2841.6 23.1 copy-start.30
  2841.6 28.8 copy-start.16
  2944.6 59.9 %copy-start.25 = (f32[11336]{0:T(1024)S(1)}, f32[11336]{0:T(1024)}, u32[]{:S(2)}) copy-start(f32[11336]{0:T(1024)} %param.30) | copy-start | bytes 136036
  (78 other events, 482.4 us)
Sparse Core Ops, SparseCore 0:
  11.5 59.9 all-gather.14
  73.7 45.2 all-gather.16
  122.5 104.7 all-gather.8
  230.7 56.3 all-gather.10
  289.1 45.2 all-gather.6
  523.2 20.7 all-gather.12
  1555.2 45.6 reduce-scatter.5
  2121.1 539.7 all-reduce.24
  2665.1 100.3 reduce-scatter.7
  2768.0 58.3 reduce-scatter.3
where the time goes:
time: 3040 us; the launch traced here: 3020 us
  waiting for transfers between devices  931 us (31%)
  local copies, waits for them, and re-layouts  699 us (23%)
  other arithmetic  578 us (19%)
  matrix products  562 us (18%)
  blocking collectives  199 us (7%)
    psum x1, waiting for transfers between devices, body(): lax.psum((term_z, term_x, term_bc, term_dt, term_out, small_term), ('seq'...  514 us
    dynamic_update_slice x64, local copies, waits for them, and re-layouts, scan_ssd(): final_state, outputs = lax.scan(stepper, initial_state, input_values)  330 us
    unnamed x6, other arithmetic  225 us
    another operation x128, other arithmetic  183 us
    all_to_all x1, waiting for transfers between devices, body(): lax.all_to_all(proj_rows, 'seq', split_axis=0, concat_axis=1, tiled=True)[0]  128 us
    all_to_all x1, waiting for transfers between devices, body(): lax.all_to_all(d_whole[None], 'seq', split_axis=1, concat_axis=0, tiled=T...  128 us
    unnamed x201, local copies, waits for them, and re-layouts  122 us
    dot_general x15, matrix products, newton_schulz(): jnp.einsum('bij,bjk->bik', poly, matrix, precision=HIGH)  119 us
  transfers between devices with their start and end apart: 14, of which 8 were waited for; matrix products, arithmetic and copies ran while one was open for 25% of the time, Pallas kernels for 0%

commit v1 on v0

v1 whole, which is shorter than its diff:
```python
import math

import jax
import jax.numpy as jnp
from jax import lax
from jax.sharding import PartitionSpec as P

D = 768
H = 24
HP = 64
NS = 128
CONV = 4
SPAN = 256
DI = 1536
XC = 1792


EPS = 1e-05
HIGH = lax.Precision.HIGHEST
MOMENTUM = 0.95
RATE = 0.2
DECAY = 0.1
SMALL_MOMENTUM = 0.9
SMALL_RATE = 0.1
COEF_A = 3.4445
COEF_B = -4.775
COEF_C = 2.0315


def kind_lengths():
    return (D, CONV * XC, XC, H, H, H, DI)


def unpack(smalls):
    pieces = []
    offset = 0
    for length in kind_lengths():
        pieces.append(smalls[offset : offset + length])
        offset = offset + length
    norm_gain, conv_flat, conv_bias, log_rates, skip_factor, step_bias, gate_gain = pieces
    return (
        norm_gain,
        conv_flat.reshape(CONV, XC),
        conv_bias,
        log_rates,
        skip_factor,
        step_bias,
        gate_gain,
    )


@jax.custom_vjp
def low(values):
    return lax.reduce_precision(values, 8, 7)


low.defvjp(lambda values: (low(values), None), lambda kept, grad: (grad,))


def intra(cumul, x_dt, b_mat, c_mat):
    size = cumul.shape[-1]
    scores = jnp.einsum("scin,scjn->scij", c_mat, b_mat)
    causal = jnp.arange(size)[:, None] >= jnp.arange(size)[None, :]
    differ = cumul[..., :, None] - cumul[..., None, :]
    decays = jnp.exp(jnp.where(causal, differ, -jnp.inf)) * scores[:, :, None]
    return jnp.einsum("schij,schjp->schip", decays, x_dt)


def prefixes(states, decay):
    running = jnp.zeros(states.shape[1:], jnp.float32)
    befores = []
    for place in range(states.shape[0]):
        befores.append(running.astype(jnp.bfloat16))
        running = running * decay[place][:, :, None] + states[place].astype(jnp.float32)
    return jnp.stack(befores)


def carry_over(c_mat, states, cumul):
    carried = jnp.einsum("scin,scfn->scif", c_mat, states)
    return carried.reshape(cumul.shape + (HP,)) * jnp.exp(cumul)[..., None]


def incoming_states(local_state, log_decay):
    n_seq = lax.axis_size("seq")
    rows = local_state.shape[1] // n_seq
    states = lax.all_to_all(
        local_state.astype(jnp.bfloat16)[None], "seq", split_axis=2, concat_axis=0, tiled=True
    )
    decay = jnp.repeat(jnp.exp(lax.all_gather(log_decay, "seq")), HP, axis=-1)
    decay = lax.dynamic_slice_in_dim(decay, lax.axis_index("seq") * rows, rows, 2)
    befores = jax.checkpoint(prefixes)(states, decay)
    return lax.all_to_all(befores, "seq", split_axis=0, concat_axis=2, tiled=True)[0]


def mixer(xbc, timesteps, conv_weight, conv_bias, log_rates, skip_factor, step_bias):
    count, length, _ = timesteps.shape
    running = conv_bias + conv_weight[0] * xbc[:, 0:length]
    for offset in range(1, CONV):
        running = running + conv_weight[offset] * xbc[:, offset : offset + length]
    act = jax.nn.silu(running)
    size = min(SPAN, length)
    chunks = length // size
    x_conv = act[:, :, :DI].reshape(count, chunks, size, H, HP)
    bc_conv = low(act[:, :, DI:]).reshape(count, chunks, size, 2 * NS)
    b_mat = bc_conv[..., :NS]
    c_mat = bc_conv[..., NS:]
    steps_dt = jax.nn.softplus(timesteps + step_bias).reshape(count, chunks, size, H)
    rates = -jnp.exp(log_rates)
    lower = jnp.tril(jnp.ones((size, size), jnp.float32))
    cumul = jnp.einsum("ij,scjh->scih", lower, steps_dt * rates, precision=HIGH)
    x_dt = x_conv * steps_dt[..., None]
    inner = jax.checkpoint(intra)(
        cumul.transpose(0, 1, 3, 2), x_dt.transpose(0, 1, 3, 2, 4), b_mat, c_mat
    ).transpose(0, 1, 3, 2, 4)
    last = cumul[:, :, -1]
    tails = jnp.exp(last[:, :, None] - cumul)
    fresh = jnp.einsum("scjf,scjn->scfn", (x_dt * tails[..., None]).reshape(count, chunks, size, DI), b_mat)
    chunk_decay = jnp.repeat(jnp.exp(last), HP, axis=-1)[..., None]
    local_state = fresh[:, 0]
    for chunk in range(1, chunks):
        local_state = local_state * chunk_decay[:, chunk] + fresh[:, chunk]
    state = incoming_states(local_state, jnp.sum(last, axis=1)).astype(jnp.float32)
    befores = []
    for chunk in range(chunks):
        befores.append(state.astype(jnp.bfloat16))
        state = state * chunk_decay[:, chunk] + fresh[:, chunk]
    carried = jax.checkpoint(carry_over)(c_mat, jnp.stack(befores, axis=1).astype(jnp.float32), cumul)
    mixed = inner + carried + skip_factor[:, None] * x_conv
    return mixed.reshape(count, length, DI)


def newton_schulz(batch):
    norms = jnp.sqrt(jnp.sum(batch * batch, axis=(1, 2), keepdims=True))
    matrix = batch / (norms + 1e-07)
    for sweep_index in range(5):
        gram = jnp.einsum("bik,bjk->bij", matrix, matrix, precision=HIGH)
        poly = COEF_B * gram + COEF_C * jnp.einsum("bij,bjk->bik", gram, gram, precision=HIGH)
        matrix = COEF_A * matrix + jnp.einsum("bij,bjk->bik", poly, matrix, precision=HIGH)
    return matrix


def small_step(params, moment):
    pieces = []
    offset = 0
    for length in kind_lengths():
        segment = moment[offset : offset + length]
        pieces.append(segment * lax.rsqrt(jnp.mean(segment * segment) + 1e-06))
        offset = offset + length
    return params - SMALL_RATE * jnp.concatenate(pieces)


def place_in(shape, piece, corner):
    return lax.dynamic_update_slice(jnp.zeros(shape, jnp.float32), piece, corner)


def body(
    block_input,
    cotangent,
    w_z,
    w_x,
    w_bc,
    w_dt,
    w_out,
    mom_z,
    mom_x,
    mom_bc,
    mom_dt,
    mom_out,
    small_params,
    small_moment,
):
    both = ("seq", "head")
    n_seq = lax.axis_size("seq")
    n_head = lax.axis_size("head")
    n_all = n_seq * n_head
    flat_idx = lax.axis_index(both)
    zero_idx = jnp.int32(0)
    low_type = jnp.bfloat16
    count, length, _ = block_input.shape
    norm_gain, conv_taps, conv_bias, log_rates, skip_factor, step_bias, gate_gain = unpack(
        small_params
    )

    def gather(matrix):
        return lax.all_gather(matrix.astype(low_type), both, axis=0, tiled=True)

    full_xbd = gather(jnp.concatenate([w_x, w_bc, w_dt], axis=1))
    full_z = gather(w_z)
    full_out = gather(w_out)
    inv_rms = lax.rsqrt(jnp.mean(block_input * block_input, axis=-1, keepdims=True) + EPS)
    unit = block_input * inv_rms
    normed = (unit * norm_gain).astype(low_type)
    cot_low = cotangent.astype(low_type)
    edge = CONV - 1
    halo = lax.ppermute(
        normed[:, length - edge :], "seq", [(place, place + 1) for place in range(n_seq - 1)]
    )

    def matmul(rows, matrix):
        return jnp.einsum("slk,kc->slc", rows, matrix, preferred_element_type=jnp.float32)

    proj_xbd = lax.optimization_barrier(matmul(normed, full_xbd).astype(low_type))
    proj_halo = lax.optimization_barrier(matmul(halo, full_xbd[:, :XC]).astype(low_type))
    proj_z = lax.optimization_barrier(matmul(normed, full_z).astype(low_type))
    xbc = jnp.concatenate([proj_halo, proj_xbd[:, :, :XC]], axis=1).astype(jnp.float32)
    timesteps = proj_xbd[:, :, XC:].astype(jnp.float32)
    mixed, mixed_pull = jax.vjp(
        mixer, xbc, timesteps, conv_taps, conv_bias, log_rates, skip_factor, step_bias
    )
    z_part = proj_z.astype(jnp.float32)
    z_sig = jax.nn.sigmoid(z_part)
    z_act = z_part * z_sig
    gated = mixed * z_act
    inv_gate = lax.rsqrt(jnp.mean(gated * gated, axis=-1, keepdims=True) + EPS)
    outgate = (gated * inv_gate * gate_gain).astype(low_type)
    block_output = block_input + matmul(outgate, full_out)
    grad_out = jnp.einsum("slc,slk->ck", outgate, cot_low, preferred_element_type=jnp.float32)
    sum_out = lax.psum_scatter(
        grad_out.astype(low_type), both, scatter_dimension=0, tiled=True
    ).astype(jnp.float32)
    mom_out_new = MOMENTUM * mom_out + sum_out
    d_gate = lax.optimization_barrier(
        jnp.einsum("slk,ck->slc", cot_low, full_out, preferred_element_type=jnp.float32).astype(
            low_type
        )
    ).astype(jnp.float32)
    d_gate_gain = jnp.sum(d_gate * gated * inv_gate, axis=(0, 1))
    d_scaled = d_gate * gate_gain
    inner = jnp.mean(d_scaled * gated, axis=-1, keepdims=True)
    d_gated = inv_gate * d_scaled - gated * inv_gate**3 * inner
    d_z = (d_gated * mixed * (z_sig + z_act * (1.0 - z_sig))).astype(low_type)
    rows_in = mom_z.shape[0]
    rows_out = mom_out.shape[0]
    in_at = flat_idx * rows_in
    out_at = flat_idx * rows_out

    def in_grad(d_part, moment):
        grad = jnp.einsum("slc,slk->ck", d_part, normed, preferred_element_type=jnp.float32)
        return grad + place_in(grad.shape, MOMENTUM * moment.T, (zero_idx, in_at))

    mom_z_rows = lax.psum_scatter(
        in_grad(d_z, mom_z).astype(low_type), both, scatter_dimension=0, tiled=True
    ).astype(jnp.float32)
    d_xbc, d_dt, d_taps, d_bias, d_rates, d_skip, d_stepb = mixed_pull(d_gated * z_act)
    d_halo = lax.ppermute(
        d_xbc[:, :edge], "seq", [(place + 1, place) for place in range(n_seq - 1)]
    )
    d_xbc = d_xbc[:, edge:] + jnp.pad(d_halo, ((0, 0), (length - edge, 0), (0, 0)))
    d_xbc = d_xbc.astype(low_type)
    d_dt = d_dt.astype(low_type)
    mom_x_rows = lax.psum_scatter(
        in_grad(d_xbc[:, :, :DI], mom_x).astype(low_type), both, scatter_dimension=0, tiled=True
    ).astype(jnp.float32)
    d_bcdt = jnp.concatenate([d_xbc[:, :, DI:], d_dt], axis=-1)
    sum_bcdt = lax.psum(in_grad(d_bcdt, jnp.concatenate([mom_bc, mom_dt], axis=1)), both)
    d_xbd = jnp.concatenate([d_xbc, d_dt], axis=-1)
    d_normed = jnp.einsum(
        "slc,kc->slk", d_z, full_z, preferred_element_type=jnp.float32
    ) + jnp.einsum("slc,kc->slk", d_xbd, full_xbd, preferred_element_type=jnp.float32)
    d_norm_gain = jnp.sum(d_normed * unit, axis=(0, 1))
    d_unit = d_normed * norm_gain
    input_grad = cotangent + inv_rms * (
        d_unit - unit * jnp.mean(d_unit * unit, axis=-1, keepdims=True)
    )
    sum_small = lax.psum(
        jnp.concatenate(
            [d_norm_gain, d_taps.reshape(-1), d_bias, d_rates, d_skip, d_stepb, d_gate_gain]
        ),
        both,
    )
    factor = 0.2 * math.sqrt(D)
    keep = 1.0 - RATE * DECAY
    if (rows_out * n_head) % HP == 0:
        axes, own_at = "head", lax.axis_index("head") * rows_out
    else:
        axes, own_at = both, out_at
    shares = jnp.stack([mom_z_rows, mom_x_rows, mom_out_new])
    blocks = lax.all_gather(shares, axes, axis=1, tiled=True)
    heads_here = blocks.shape[1] // HP
    sum_bc = sum_bcdt[: 2 * NS]
    sum_dt = sum_bcdt[2 * NS :]
    batch = jnp.concatenate(
        [
            blocks.reshape(3 * heads_here, HP, D),
            jnp.pad(sum_dt, ((0, HP - H), (0, 0)))[None],
        ]
    )
    ortho = newton_schulz(batch)
    ortho_dt = ortho[-1, :H].T
    ortho_bc = newton_schulz(sum_bc[None])[0].T
    ortho = lax.dynamic_slice_in_dim(
        ortho[:-1].reshape(3, heads_here * HP, D), own_at, rows_out, 1
    )
    back = jnp.stack([mom_z_rows, mom_x_rows, ortho[0], ortho[1]]).astype(low_type)
    back = back.reshape(4, rows_out, n_all, rows_in).transpose(2, 0, 3, 1)
    back = lax.all_to_all(back, both, split_axis=0, concat_axis=0, tiled=True)
    back = back.transpose(1, 2, 0, 3).reshape(4, rows_in, DI).astype(jnp.float32)

    def own_rows(matrix):
        return lax.dynamic_slice_in_dim(matrix, in_at, rows_in, 0)

    new_w_z = w_z * keep - RATE * factor * back[2]
    new_w_x = w_x * keep - RATE * factor * back[3]
    new_w_bc = w_bc * keep - RATE * factor * own_rows(ortho_bc)
    new_w_dt = w_dt * keep - RATE * factor * own_rows(ortho_dt)
    new_w_out = w_out * keep - RATE * factor * ortho[2]
    new_small_moment = SMALL_MOMENTUM * small_moment + sum_small
    new_small_params = small_step(small_params, new_small_moment)
    return (
        block_output,
        input_grad,
        new_w_z,
        new_w_x,
        new_w_bc,
        new_w_dt,
        new_w_out,
        back[0],
        back[1],
        own_rows(sum_bc.T),
        own_rows(sum_dt.T),
        mom_out_new,
        new_small_moment,
        new_small_params,
    )


def solution(mesh):
    return jax.shard_map(
        body,
        mesh=mesh,
        in_specs=(
            P("head", "seq", None),
            P("head", "seq", None),
            P(("seq", "head"), None),
            P(("seq", "head"), None),
            P(("seq", "head"), None),
            P(("seq", "head"), None),
            P(("seq", "head"), None),
            P(("seq", "head"), None),
            P(("seq", "head"), None),
            P(("seq", "head"), None),
            P(("seq", "head"), None),
            P(("seq", "head"), None),
            P(),
            P(),
        ),
        out_specs=(
            P("head", "seq", None),
            P("head", "seq", None),
            P(("seq", "head"), None),
            P(("seq", "head"), None),
            P(("seq", "head"), None),
            P(("seq", "head"), None),
            P(("seq", "head"), None),
            P(("seq", "head"), None),
            P(("seq", "head"), None),
            P(("seq", "head"), None),
            P(("seq", "head"), None),
            P(("seq", "head"), None),
            P(),
            P(),
        ),
        check_vma=False,
    )
```

time: 3040 us -> 938 us (0.31)
  waiting for transfers between devices: 931 us -> 287 us
  local copies, waits for them, and re-layouts: 699 us -> 181 us
  other arithmetic: 578 us -> 161 us
  matrix products: 562 us -> 164 us
  blocking collectives: 199 us -> 84.7 us
    psum x1, waiting for transfers between devices: 514 us -> 118 us  [body(): lax.psum(in_grad(d_bcdt, jnp.concatenate([mom_bc, mom_dt], axis=1)), both)]
    dynamic_update_slice x64 -> x1, local copies, waits for them, and re-layouts: 330 us -> 0.27 us  [incoming_states(): lax.dynamic_slice_in_dim(decay, lax.axis_index('seq') * rows, rows, 2)]
    all_to_all x4 -> x5, waiting for transfers between devices: 256 us -> 8.82 us  [the longest x1 8.81 us: body(): back = lax.all_to_all(back, both, split_axis=0, concat_axis=0, tiled=True)]
    unnamed x6 -> x8, other arithmetic: 225 us -> 5.21 us
    dot_general x230 -> x27, matrix products: 320 us -> 128 us  [the longest x3 39.1 us: intra(): return jnp.einsum('schij,schjp->schip', decays, x_dt)]
    another operation x144 -> x7, other arithmetic: 183 us -> 5.09 us
    all_gather x2 -> x1, blocking collectives: 137 us -> 21.1 us  [incoming_states(): decay = jnp.repeat(jnp.exp(lax.all_gather(log_decay, 'seq')), HP, axis=-1)]
    dot_general x15 -> x10, matrix products: 119 us -> 14 us  [newton_schulz(): jnp.einsum('bij,bjk->bik', poly, matrix, precision=HIGH)]
  transfers between devices with their start and end apart: 14 -> 15, of which waited for: 8 -> 5; matrix products, arithmetic and copies ran while one was open for 25% -> 41% of each run, Pallas kernels for 0% -> 0%
where the time goes in v1:
time: 938 us; the launch traced here: 931 us
  waiting for transfers between devices  287 us (31%)
  local copies, waits for them, and re-layouts  181 us (19%)
  matrix products  164 us (17%)
  other arithmetic  161 us (17%)
  blocking collectives  84.7 us (9%)
  starting transfers between devices  31.7 us (3%)
  between operations  21.9 us (2%)
    psum x1, waiting for transfers between devices, body(): lax.psum(in_grad(d_bcdt, jnp.concatenate([mom_bc, mom_dt], axis=1)), both)  118 us
    unnamed x11, waiting for transfers between devices  96.9 us
    all_gather x3, waiting for transfers between devices, gather(): return lax.all_gather(matrix.astype(low_type), both, axis=0, tiled=True)  50.8 us
    psum x1, blocking collectives, body(): lax.psum(jnp.concatenate([d_norm_gain, d_taps.reshape(-1), d_bias, d_rate...  40.4 us
    dot_general x3, matrix products, intra(): return jnp.einsum('schij,schjp->schip', decays, x_dt)  39.1 us
    unnamed x256, local copies, waits for them, and re-layouts  36.5 us
    reshape x3, local copies, waits for them, and re-layouts, mixer(): x_conv = act[:, :, :DI].reshape(count, chunks, size, H, HP)  23.8 us
    unnamed x1, blocking collectives  23.3 us
  transfers between devices with their start and end apart: 15, of which 5 were waited for; matrix products, arithmetic and copies ran while one was open for 41% of the time, Pallas kernels for 0%

profile of v1, /device:TPU:0, one launch (start us, length us, event | category | flops | bytes accessed | tf_op | source)
XLA Modules:
  0.0 930.5 jit_solution(13393112907380199872)
XLA Ops:
  22.2 50.8 %all-gather.7.cloned.1.call-done = bf16[768,1816]{1,0:T(8,128)(2,1)} async-done(((bf16[24,1816]{1,0:T(8,128)(2,1)}), bf16[768,1816]{1,0:T(8,128)(2,1)}) %all-gather.7.cloned.1.call-update) | async-done | bytes 2789392 | tf_op jit(solution)/shard_map/all_gather | solution.py:185
  90.4 7.4 copy.649
  103.1 9.1 fusion.24
  135.9 7.6 fusion.182
  165.5 21.1 %all-gather.1 = f32[8,2,24]{2,1,0:T(2,128)S(1)} all-gather(f32[1,2,24]{2,1,0:T(2,128)S(1)} %bitcast.656), channel_id=2, replica_groups=mesh['seq'=8,'head'=4] {'seq'}, dimensions={0}, use_global_device_ids=true | all-gather | bytes 1728 | tf_op jit(solution)/shard_map/jvp()/all_gather | solution.py:89
  207.0 8.2 reshape.797
  243.6 8.2 copy.668
  251.8 9.1 reshape.802
  277.4 10.6 %multiply_reduce_fusion.5 = (f32[1536]{0:T(1024)S(1)}, f32[2,512,1536]{1,2,0:T(8,128)}, bf16[2,512,1536]{1,2,0:T(8,128)(2,1)}) fusion(f32[2,512,1792]{1,2,0:T(8,128)} %copy-done.2, bf16[2,512,1536]{1,2,0:T(8,128)(2,1)S(1)} %copy-done.15, f32[2,512]{1,0:T(2,128)S(1)} %broadcast_multiply_fusion.6, f32[2,512,1536]{1,2,0:T(8,128)S(1)} %copy-done.4, ...), kind=kLoop, calls=%fused_computation.53 | loop fusion | flops 31455744 | bytes 34627584 | tf_op jit(solution)/shard_map/transpose(jvp())/reduce_sum | solution.py:128
  288.0 8.2 reshape.803
  346.8 16.2 %fusion.8 = (f32[2,2,24,256]{3,2,1,0:T(8,128)}, f32[2,2,24,256]{3,2,1,0:T(8,128)}, bf16[2,2,256,256]{3,2,1,0:T(8,128)(2,1)S(1)}) fusion(f32[2,2,256,256]{3,2,1,0:T(8,128)} %fusion.207, f32[2,2,24,256]{3,2,1,0:T(8,128)S(1)} %copy-done.67, pred[256,256]{1,0:T(8,128)(4,1)} %iota_compare_fusion, bf16[2,2,24,256,64]{3,4,2,1,0:T(8,128)(2,1)S(1)} %bitcast.629, ...), kind=kOutput, calls=%fused_computation.11 | convolution fusion | flops 861618176 | bytes 8224768 | tf_op jit(solution)/shard_map/transpose(jvp(jvp()))/checkpoint/schij,schjp->schip/dot_general | solution.py:66
  395.6 23.3 %all-reduce.34 = f32[8,2,24]{2,1,0:T(2,128)S(1)} all-reduce(f32[8,2,24]{2,1,0:T(2,128)S(1)} %bitcast.648), channel_id=3, replica_groups=mesh['seq'=8,'head'=4] {'seq'}, use_global_device_ids=true, to_apply=%region_16.17.clone | all-reduce | flops 384 | bytes 3072
  425.2 7.6 fusion.79
  436.7 15.5 %multiply_reduce_fusion.6 = (f32[2,2,256,24]{2,3,1,0:T(8,128)}, f32[2,2,256,24]{2,3,1,0:T(8,128)}, f32[2,2,256,24,64]{2,4,3,1,0:T(8,128)}) fusion(f32[2,2,256,24,64]{2,4,3,1,0:T(8,128)} %bitcast.622, f32[2,2,256,24,64]{2,1,4,3,0:T(2,128)} %reshape.797, f32[2,2,256,24]{2,3,1,0:T(8,128)S(1)} %bitcast.640, f32[2,2,256,24,64]{2,1,4,3,0:T(2,128)} %reshape.803, ...), kind=kOutput, calls=%fused_computation.54 | convolution fusion | flops 839860224 | bytes 29917280 | tf_op jit(solution)/shard_map/transpose(jvp(jvp()))/checkpoint/schij,schjp->schip/dot_general | solution.py:66
  452.2 11.0 %copy.689 = f32[2,2,256,24,64]{2,1,4,3,0:T(2,128)} copy(f32[2,2,256,24,64]{2,4,3,1,0:T(8,128)} %get-tuple-element.191) | data formatting | bytes 12582912 | tf_op jit(solution)/shard_map/transpose(jvp())/add_any | solution.py:111
  463.3 9.0 reshape.807
  472.3 22.4 %multiply_reduce_fusion.4 = (f32[1792]{0:T(1024)S(1)}, f32[1792]{0:T(1024)S(1)}, f32[1792]{0:T(1024)S(1)}, f32[1792]{0:T(1024)S(1)}, f32[1792]{0:T(1024)}, /*index=5*/f32[2,512,1792]{1,2,0:T(8,128)}) fusion(f32[2,515,1792]{1,2,0:T(8,128)} %copy-done, f32[2,512,1792]{1,2,0:T(8,128)} %get-tuple-element.185, f32[2,512,1536]{1,2,0:T(8,128)} %reshape.807, ...), kind=kLoop, calls=%fused_computation.37 | loop fusion | flops 34856192 | bytes 51416064 | tf_op jit(solution)/shard_map/transpose(jvp())/reduce_sum | solution.py:99
  494.7 8.6 broadcast_multiply_fusion
  507.9 11.6 %pad_add_fusion = f32[2,515,1792]{1,2,0:T(8,128)} fusion(f32[2,512,1792]{1,2,0:T(8,128)S(1)} %get-tuple-element.188, f32[2,512,1792]{1,2,0:T(8,128)S(1)} %copy-done.1, f32[2,512,1792]{1,2,0:T(8,128)} %get-tuple-element.190, f32[2,512,1792]{1,2,0:T(8,128)S(1)} %get-tuple-element.187), kind=kLoop, calls=%fused_computation.23 | loop fusion | flops 5537280 | bytes 36743168 | tf_op jit(solution)/shard_map/transpose(jvp())/add_any | solution.py:97
  551.9 40.4 %psum.15 = f32[11336]{0:T(1024)S(1)} all-reduce(f32[11336]{0:T(1024)S(1)} %concatenate.33), channel_id=1, replica_groups=mesh['seq'=8,'head'=4] {'seq','head'}, use_global_device_ids=true, to_apply=%region_41.42 | all-reduce | flops 11336 | bytes 90688 | tf_op jit(solution)/shard_map/psum | solution.py:265
  626.8 118.3 %all-reduce.37.cloned.1.call-done = f32[280,768]{1,0:T(8,128)} async-done(((f32[280,768]{1,0:T(8,128)}), f32[280,768]{1,0:T(8,128)}) %all-reduce.37.cloned.1.call-update) | async-done | bytes 860176 | tf_op jit(solution)/shard_map/psum | solution.py:255
  753.4 96.1 %reduce-scatter.12.cloned.1.call-done = bf16[48,768]{1,0:T(8,128)(2,1)} async-done(((bf16[1536,768]{1,0:T(8,128)(2,1)}), bf16[48,768]{1,0:T(8,128)(2,1)}) %reduce-scatter.12.cloned.1.call-update) | async-done | bytes 73744
  861.0 12.1 %all-gather.13.cloned.1.call-done = f32[3,192,768]{2,1,0:T(8,128)} async-done(((f32[3,48,768]{2,1,0:T(8,128)}), f32[3,192,768]{2,1,0:T(8,128)}) %all-gather.13.cloned.1.call-update) | async-done | bytes 1769488 | tf_op jit(solution)/shard_map/all_gather | solution.py:278
  910.3 8.8 all-to-all-done.4
  (529 shorter events, 367.3 us)
Async XLA Ops:
  7.2 65.8 %all-gather.7.cloned.1.call-start = ((), (), s32[]{:S(2)}) async-start(), calls=%async_computation.8 | async-start | bytes 3041280 | tf_op jit(solution)/shard_map/all_gather | solution.py:185
  10.4 148.0 %all-gather.11.cloned.1.call-start = ((), (), s32[]{:S(2)}) async-start(), calls=%async_computation.10 | async-start | bytes 2433024 | tf_op jit(solution)/shard_map/all_gather | solution.py:185
  12.1 188.4 %all-gather.9.cloned.1.call-start = ((), (), s32[]{:S(2)}) async-start(), calls=%async_computation.9 | async-start | bytes 2433024 | tf_op jit(solution)/shard_map/all_gather | solution.py:185
  15.0 63.4 %copy-start.93 = (f32[2,512]{1,0:T(2,128)}, f32[2,512]{1,0:T(2,128)S(1)}, u32[]{:S(2)}) copy-start(f32[2,512]{1,0:T(2,128)S(1)} %add_rsqrt_fusion.1) | copy-start | bytes 12292
  16.6 81.3 %collective-permute-start = (bf16[2,3,768]{2,1,0:T(4,128)(2,1)S(1)}, bf16[2,3,768]{2,1,0:T(4,128)(2,1)S(1)}, u32[]{:S(2)}, u32[]{:S(2)}) collective-permute-start(bf16[2,3,768]{2,1,0:T(4,128)(2,1)S(1)} %slice.325), channel_id=1, source_target_pairs={{0,4},{4,8},{8,12},{12,16},{16,20},{20,24},{24,28},{1,5},{5,9},{9,... | collective-permute-start | bytes 27656 | tf_op jit(solution)/shard_map/ppermute | solution.py:195
  22.2 56.3 %copy-start.103 = (f32[24]{0:T(128)}, f32[24]{0:T(128)S(1)}, u32[]{:S(2)}) copy-start(f32[24]{0:T(128)S(1)} %get-tuple-element.227) | copy-start | bytes 292
  22.2 56.4 %copy-start.106 = (f32[24]{0:T(128)}, f32[24]{0:T(128)S(1)}, u32[]{:S(2)}) copy-start(f32[24]{0:T(128)S(1)} %get-tuple-element.226) | copy-start | bytes 292
  22.2 80.9 %copy-start.77 = (f32[1792]{0:T(1024)}, f32[1792]{0:T(1024)S(1)}, u32[]{:S(2)}) copy-start(f32[1792]{0:T(1024)S(1)} %get-tuple-element.229) | copy-start | bytes 21508
  22.2 80.9 %copy-start.79 = (f32[1792]{0:T(1024)}, f32[1792]{0:T(1024)S(1)}, u32[]{:S(2)}) copy-start(f32[1792]{0:T(1024)S(1)} %get-tuple-element.230) | copy-start | bytes 21508
  22.2 80.9 %copy-start.81 = (f32[1792]{0:T(1024)}, f32[1792]{0:T(1024)S(1)}, u32[]{:S(2)}) copy-start(f32[1792]{0:T(1024)S(1)} %get-tuple-element.231) | copy-start | bytes 21508
  22.2 80.9 %copy-start.83 = (f32[1792]{0:T(1024)}, f32[1792]{0:T(1024)S(1)}, u32[]{:S(2)}) copy-start(f32[1792]{0:T(1024)S(1)} %get-tuple-element.232) | copy-start | bytes 21508
  87.0 148.7 %copy-start.46 = (f32[2,3,2,8,256]{4,3,1,2,0:T(8,128)}, f32[2,3,2,8,256]{4,3,1,2,0:T(8,128)S(1)}, u32[]{:S(2)}) copy-start(f32[2,3,2,8,256]{4,3,1,2,0:T(8,128)S(1)} %copy.840) | copy-start | bytes 294916
  143.5 88.3 %copy-start.9 = (f32[2,2,1536,128]{2,3,1,0:T(8,128)}, f32[2,2,1536,128]{2,3,1,0:T(8,128)S(1)}, u32[]{:S(2)}) copy-start(f32[2,2,1536,128]{2,3,1,0:T(8,128)S(1)} %fusion.182) | copy-start | bytes 9437188
  148.0 40.8 %all-to-all-start = ((bf16[1,2,1536,128]{3,1,0,2:T(2,128)(2,1)}), bf16[1,2,1536,128]{3,1,0,2:T(2,128)(2,1)}, u32[]{:S(2)}, u32[]{:S(2)}) async-start(bf16[1,2,1536,128]{3,1,0,2:T(2,128)(2,1)} %copy.653), calls=%async_computation | async-start | bytes 1572864 | tf_op jit(solution)/shard_map/jvp()/all_to_all | solution.py:86
  196.2 31.3 %all-to-all-start.1 = ((bf16[8,2,192,128]{3,2,1,0:T(8,128)(2,1)}), bf16[8,2,192,128]{3,2,1,0:T(8,128)(2,1)}, u32[]{:S(2)}, u32[]{:S(2)}) async-start(bf16[8,2,192,128]{3,2,1,0:T(8,128)(2,1)} %fusion.146), calls=%async_computation.1 | async-start | bytes 1572864 | tf_op jit(solution)/shard_map/jvp()/all_to_all | solution.py:92
  200.4 423.1 %reduce-scatter.14.cloned.1.call-start = ((), (), s32[]{:S(2)}) async-start(), calls=%async_computation.15 | async-start | bytes 2433024
  319.1 63.3 %all-to-all-start.2 = ((bf16[1,2,1536,128]{3,1,0,2:T(2,128)(2,1)}), bf16[1,2,1536,128]{3,1,0,2:T(2,128)(2,1)}, u32[]{:S(2)}, u32[]{:S(2)}) async-start(bf16[1,2,1536,128]{3,1,0,2:T(2,128)(2,1)} %copy.679), calls=%async_computation.2 | async-start | bytes 1572864 | tf_op jit(solution)/shard_map/transpose(jvp())/all_to_all | solution.py:92
  324.9 300.6 %reduce-scatter.10.cloned.1.call-start = ((), (), s32[]{:S(2)}) async-start(), calls=%async_computation.13 | async-start | bytes 2433024
  385.3 34.8 %all-to-all-start.3 = ((bf16[8,2,192,128]{3,2,1,0:T(8,128)(2,1)}), bf16[8,2,192,128]{3,2,1,0:T(8,128)(2,1)S(1)}, u32[]{:S(2)}, u32[]{:S(2)}) async-start(bf16[8,2,192,128]{3,2,1,0:T(8,128)(2,1)} %pad_add_fusion.4), calls=%async_computation.3 | async-start | bytes 1572864 | tf_op jit(solution)/shard_map/transpose(jvp())/all_to_all | solution.py:86
  391.2 353.9 %all-reduce.37.cloned.1.call-start = ((), (), s32[]{:S(2)}) async-start(), calls=%async_computation.12 | async-start | bytes 1720320 | tf_op jit(solution)/shard_map/psum | solution.py:255
  524.6 11.0 %collective-permute-start.1 = (f32[2,3,1792]{2,0,1:T(2,128)}, f32[2,3,1792]{2,0,1:T(2,128)}, u32[]{:S(2)}, u32[]{:S(2)}) collective-permute-start(f32[2,3,1792]{2,0,1:T(2,128)} %copy.690), channel_id=1, source_target_pairs={{4,0},{8,4},{12,8},{16,12},{20,16},{24,20},{28,24},{5,1},{9,5},{13... | collective-permute-start | bytes 129032 | tf_op jit(solution)/shard_map/ppermute | solution.py:245
  616.6 232.9 %reduce-scatter.12.cloned.1.call-start = ((), (), s32[]{:S(2)}) async-start(), calls=%async_computation.14 | async-start | bytes 2433024
  617.3 255.7 %all-gather.13.cloned.1.call-start = ((), (), s32[]{:S(2)}) async-start(), calls=%async_computation.11 | async-start | bytes 2211840 | tf_op jit(solution)/shard_map/all_gather | solution.py:278
  902.9 16.2 %all-to-all-start.4 = ((bf16[32,2,2304]{2,1,0:T(2,128)(2,1)}), bf16[32,2,2304]{2,1,0:T(2,128)(2,1)S(1)}, u32[]{:S(2)}, u32[]{:S(2)}) async-start(bf16[32,2,2304]{2,1,0:T(2,128)(2,1)} %reshape.869), calls=%async_computation.4 | async-start | bytes 589824 | tf_op jit(solution)/shard_map/all_to_all | solution.py:296
  (109 other events, 816.7 us)
Sparse Core Ops, SparseCore 0:
  11.4 61.5 all-gather.6
  76.5 56.0 all-gather.10
  135.5 60.2 all-gather.8
  303.5 103.6 reduce-scatter.13
  413.2 97.0 reduce-scatter.9
  616.7 128.3 all-reduce.36
  750.4 99.0 reduce-scatter.11
  853.3 19.7 all-gather.12
